TPU v7x, 256 devices: a whole 4x4x8 slice. The times are simulated.
256 devices in a mesh: lat: 64 (over y_lo, x, z), lev: 4 (over y_hi, core).
Axes of the slice: x: 4, y: 4 (y_hi: 2, y_lo: 2; y = y_hi * 2 + y_lo), z: 8, core: 2. Of those that a mesh axis runs over, the one named last changes fastest.
Arguments:
- zonal_velocity: float32 [16, 256, 2880], P('lev', 'lat'), may hold values from -1 to 1
- meridional_velocity: float32 [16, 256, 2880], P('lev', 'lat'), may hold values from -1 to 1
- heat_anomaly: float32 [16, 256, 2880], P('lev', 'lat'), may hold values from -6 to 6
- layer_pressure_depth: float32 [16, 256, 2880], P('lev', 'lat'), may hold values from 0.8 to 1.2
- reference_layer_shares: float32 [16], replicated, may hold values from 0.5 to 2
Outputs:
- temp_remapped: float32 [16, 256, 2880], P(None, 'lat', 'lev')
- u_remapped: float32 [16, 256, 2880], P(None, 'lat', 'lev')
- v_remapped: float32 [16, 256, 2880], P(None, 'lat', 'lev')
- thick_remapped: float32 [16, 256, 2880], P(None, 'lat', 'lev')
All inputs are finite; a program needn't handle non-finite values.
Results may differ from a plain program's by a relative error of at most 0.0003.
Values sent between devices are 32-bit elements; how exact they have to be, the bound alone decides.
A program may use at most 192 MiB of HBM per device.

v0:
```python
import math

import jax
import jax.numpy as jnp
import numpy as np
from jax import lax
from jax.experimental import pallas as pl
from jax.experimental.pallas import tpu as pltpu
from jax.sharding import PartitionSpec as P

SPEED = 0.04
QUARTER = math.cos(math.pi / 4.0)
SPACING = 180.0 / 1440.0
LON = 2880
ROWS = 4
LEVELS = 4
GROUPS = 4
COARSE = 12
FINE = 240
WIDE = 256
EDGE = 8
PER = COARSE // GROUPS
WAVES = COARSE // 2 + 1
MESH = pl.DeviceIdType.MESH


def grid_table(bands):
    f32 = np.float32
    rows = np.arange(bands * ROWS)
    faces = np.arange(bands * ROWS + 1)
    scale = f32(math.pi / 180.0)
    center = np.cos(((rows.astype(f32) + f32(0.5)) * f32(SPACING) - f32(90.0)) * scale)
    face = np.cos((faces.astype(f32) * f32(SPACING) - f32(90.0)) * scale)
    face = np.where(faces == 0, f32(0.0), face)
    table = np.zeros((bands, 16), f32)
    for band in range(bands):
        at = band * ROWS
        table[band, 0:4] = f32(1.0) / center[at : at + 4]
        table[band, 4:9] = face[at : at + 5]
        table[band, 9:13] = center[at : at + 4] / f32(QUARTER)
    return table


def split_bf16(array):
    high = array.astype(jnp.bfloat16)
    low = (array - high.astype(np.float32)).astype(jnp.bfloat16)
    return high, low


def constants():
    cell = np.arange(FINE)
    wave = np.arange(FINE)
    angle = 2.0 * np.pi * (np.outer(cell, wave) % FINE) / FINE
    cos, sin = np.cos(angle), np.sin(angle)
    forward = np.zeros((2 * WIDE, 2 * WIDE))
    spots = slice(EDGE, EDGE + FINE)
    spots_im = slice(WIDE + EDGE, WIDE + EDGE + FINE)
    forward[spots, 0:FINE] = cos
    forward[spots, WIDE : WIDE + FINE] = -sin
    forward[spots_im, 0:FINE] = sin
    forward[spots_im, WIDE : WIDE + FINE] = cos
    backward = np.zeros((2 * WIDE, 2 * WIDE))
    backward[0:FINE, spots] = cos.T
    backward[0:FINE, spots_im] = sin.T
    backward[WIDE : WIDE + FINE, spots] = -sin.T
    backward[WIDE : WIDE + FINE, spots_im] = cos.T
    matrices = np.stack(
        [m for whole in (forward, backward) for m in split_bf16(whole.astype(np.float32))]
    )
    tables = np.zeros((3, 8, WIDE), np.float32)
    for order in range(WAVES):
        turn = 2.0 * np.pi * order * cell / LON
        tables[0, order, spots] = np.cos(turn)
        tables[1, order, spots] = np.sin(turn)
        number = (order + COARSE * wave).astype(np.float32)
        tables[2, order, 0:FINE] = np.sin(number * np.float32(math.pi / LON))
    return matrices, tables


def cos_of(index):
    value = math.cos(2.0 * math.pi * index / COARSE)
    return round(value) if abs(value - round(value)) < 1e-9 else round(2 * value) / 2 if abs(
        2 * value - round(2 * value)
    ) < 1e-9 else value


def combine(terms):
    total = None
    for factor, array in terms:
        if factor == 0:
            continue
        if total is None:
            total = array if factor == 1 else -array if factor == -1 else factor * array
        elif factor == 1:
            total = total + array
        elif factor == -1:
            total = total - array
        else:
            total = total + factor * array
    return total


def forward_blocks(x):
    even = {n: x[n] + x[COARSE - n] for n in range(1, 6)}
    odd = {n: x[n] - x[COARSE - n] for n in range(1, 6)}
    ends = {0: x[0] + x[6], 1: x[0] - x[6]}
    even_sum = {n: even[n] + even[6 - n] for n in (1, 2)}
    even_dif = {n: even[n] - even[6 - n] for n in (1, 2)}
    odd_sum = {n: odd[n] + odd[6 - n] for n in (1, 2)}
    odd_dif = {n: odd[n] - odd[6 - n] for n in (1, 2)}
    real, imag = [], []
    for k in range(WAVES):
        pick = even_dif if k % 2 else even_sum
        terms = [(1, ends[k % 2])] + [(cos_of(n * k), pick[n]) for n in (1, 2)]
        terms.append((cos_of(3 * k), even[3]))
        real.append(combine(terms))
        if 0 < k < 6:
            pick = odd_sum if k % 2 else odd_dif
            terms = [(-cos_of(n * k - 3), pick[n]) for n in (1, 2)]
            terms.append((-cos_of(3 * k - 3), odd[3]))
            imag.append(combine(terms))
        else:
            imag.append(None)
    return real, imag


def backward_blocks(real, imag):
    base = {0: real[0] + real[6], 1: real[0] - real[6]}
    blocks = [None] * COARSE
    for b in range(0, 7):
        cosine = combine([(1, base[b % 2])] + [(cos_of(k * b), real[k]) for k in range(1, 6)])
        if b in (0, 6):
            blocks[b] = cosine
            continue
        sine = combine([(-cos_of(k * b - 3), imag[k]) for k in range(1, 6)])
        blocks[b] = cosine + sine
        blocks[COARSE - b] = cosine - sine
    return blocks


def minmod(left, right):
    return jnp.maximum(jnp.minimum(left, right), 0.0) + jnp.minimum(jnp.maximum(left, right), 0.0)


def window(load, block):
    lane = lax.broadcasted_iota(jnp.int32, (8, WIDE), 1)
    if block == 0:
        body = pltpu.roll(load(0, 256), EDGE, 1)
        tail = pltpu.roll(load(2688, 2944), 256 - (LON - EDGE - 2688), 1)
        return jnp.where(lane < EDGE, tail, body)
    start = FINE * block - EDGE
    first = start // 128 * 128
    body = pltpu.roll(load(first, first + 384), (384 - (start - first)) % 384, 1)[:, :WIDE]
    if block == COARSE - 1:
        head = pltpu.roll(load(0, 256), WIDE - EDGE, 1)
        body = jnp.where(lane >= WIDE - EDGE, head, body)
    return body


def kernel(
    grid_ref, share_ref, u_ref, v_ref, t_ref, h_ref, mat_ref, tab_ref,
    out_ref,
    raw, cut, field, sent, held, spread, gain, z_hi, z_lo, field_out,
    halo_send, halo_recv, turn_send, turn_recv, own_sem,
):
    bands = lax.axis_size("lat")
    band = lax.axis_index("lat")
    group = lax.axis_index("lev")
    above = (lax.rem(band + 1, bands), group)
    below = (lax.rem(band + bands - 1, bands), group)
    partners = [(band, lax.rem(group + step, GROUPS)) for step in range(1, GROUPS)]

    barrier = pltpu.get_barrier_semaphore()
    for device in [above, below] + partners:
        pl.semaphore_signal(barrier, inc=1, device_id=device, device_id_type=MESH)

    for row in range(ROWS):
        raw[0, 2 + row, 0:4, 0:LON] = h_ref[:, row, :]
        raw[0, 2 + row, 4:8, 0:LON] = v_ref[:, row, :]
        raw[1, 2 + row, 0:4, 0:LON] = u_ref[:, row, :]
        raw[1, 2 + row, 4:8, 0:LON] = t_ref[:, row, :]

    pl.semaphore_wait(barrier, 2 + len(partners))

    def halo(pair, side):
        return pltpu.make_async_remote_copy(
            src_ref=raw.at[pair, pl.ds(2 if side else 4, 2)],
            dst_ref=raw.at[pair, pl.ds(6 if side else 0, 2)],
            send_sem=halo_send.at[pair, side],
            recv_sem=halo_recv.at[pair, side],
            device_id=below if side else above,
            device_id_type=MESH,
        )

    halos = [halo(pair, side) for pair in range(2) for side in range(2)]
    for copy in halos:
        copy.start()

    def cut_row(pair, row):
        def load(first, last):
            return raw[pair, row, :, first:last]

        for block in range(COARSE):
            cut[pair, row, block] = window(load, block)

    def cut_own(step, carry):
        cut_row(step // ROWS, 2 + lax.rem(step, ROWS))
        return carry

    lax.fori_loop(0, 2 * ROWS, cut_own, 0)

    sub16 = lax.broadcasted_iota(jnp.int32, (16, WIDE), 0)
    ratio = jnp.full((16, WIDE), grid_ref[band, 9])
    for row in range(1, ROWS):
        ratio = jnp.where(sub16 >= LEVELS * row, grid_ref[band, 9 + row], ratio)
    for order in range(WAVES):
        sine = jnp.broadcast_to(tab_ref[2, order : order + 1, :], (16, WIDE))
        damping = ratio / jnp.maximum(sine, ratio)
        gain[order] = damping * damping * ((1.0 if order in (0, 6) else 2.0) / LON)

    for copy in halos:
        copy.wait_recv()

    def cut_halo(step, carry):
        row = lax.rem(step, 4)
        cut_row(step // 4, row + 4 * (row // 2))
        return carry

    lax.fori_loop(0, 8, cut_halo, 0)

    has_below = jnp.where(band > 0, 1.0, 0.0)
    has_above = jnp.where(band < bands - 1, 1.0, 0.0)

    def advect(block, carry):
        low = lax.broadcasted_iota(jnp.int32, (8, WIDE), 0) < 4

        def swap(array):
            return pltpu.roll(array, 4, 0)

        quants = ([], [])
        north, east = [], []
        for row in range(8):
            first, second = cut[0, row, block], cut[1, row, block]
            if row < 2:
                first, second = first * has_below, second * has_below
            elif row > 5:
                first, second = first * has_above, second * has_above
            turned = swap(first)
            thick = jnp.where(low, first, turned)
            north.append(jnp.where(low, turned, first))
            quants[0].append(jnp.where(low, first, first * thick))
            quants[1].append(second * thick)
            if 2 <= row < 6:
                east.append(jnp.where(low, second, swap(second)))

        rolled = lambda array, step: pltpu.roll(array, step % WIDE, 1)
        zonal_c = [SPEED * (wind + rolled(wind, -1)) for wind in east]
        face_c = [SPEED * (north[face + 1] + north[face + 2]) for face in range(5)]
        updated = ([], [])
        for pair in range(2):
            q = quants[pair]
            diff = [q[row + 1] - q[row] for row in range(7)]
            slope = [None] + [minmod(diff[row - 1], diff[row]) for row in range(1, 7)]
            flux = []
            for face in range(5):
                c = face_c[face]
                up = c >= 0.0
                value = jnp.where(up, q[face + 1], q[face + 2])
                lean = jnp.where(up, slope[face + 1], slope[face + 2])
                part = jnp.where(up, 0.5, -0.5) - 0.5 * c
                flux.append(c * grid_ref[band, 4 + face] * (value + part * lean))
            for row in range(ROWS):
                own = q[row + 2]
                c = zonal_c[row]
                after = rolled(own, -1)
                step = after - own
                tilt = minmod(rolled(step, 1), step)
                up = c >= 0.0
                value = jnp.where(up, own, after)
                lean = jnp.where(up, tilt, rolled(tilt, -1))
                part = jnp.where(up, 0.5, -0.5) - 0.5 * c
                through = c * (value + part * lean)
                change = (flux[row + 1] - flux[row]) * grid_ref[band, row]
                updated[pair].append(own - (through - rolled(through, 1)) - change)
        for half in range(2):
            rows = pl.ds(8 * half, 8)
            one, two = updated[0][2 * half], updated[0][2 * half + 1]
            thick = jnp.where(low, one, swap(two))
            sent[0, block, rows] = thick
            field[0, block, rows] = jnp.where(low, swap(one), two) / thick
            one, two = updated[1][2 * half], updated[1][2 * half + 1]
            field[1, block, rows] = jnp.where(low, one, swap(two)) / thick
            field[2, block, rows] = jnp.where(low, swap(one), two) / thick
        return carry

    lax.fori_loop(0, COARSE, advect, 0)

    def turn(item, step):
        target = lax.rem(group + step, GROUPS)
        return pltpu.make_async_remote_copy(
            src_ref=sent.at[item, pl.ds(PER * target, PER)],
            dst_ref=held.at[item, group],
            send_sem=turn_send.at[item, step - 1],
            recv_sem=turn_recv.at[item, step - 1],
            device_id=(band, target),
            device_id_type=MESH,
        )

    def keep(item):
        return pltpu.make_async_copy(
            sent.at[item, pl.ds(PER * group, PER)], held.at[item, group], own_sem.at[item]
        )

    def start_turn(item):
        for step in (2, 3, 1):
            turn(item, step).start()
        keep(item).start()

    start_turn(0)

    for item in range(3):
        for tile in range(2):
            lanes = pl.ds(128 * tile, 128)
            real, imag = forward_blocks([field[item, block, :, lanes] for block in range(COARSE)])
            for order in range(WAVES):
                cos = jnp.broadcast_to(tab_ref[0, order : order + 1, lanes], (16, 128))
                sin = jnp.broadcast_to(tab_ref[1, order : order + 1, lanes], (16, 128))
                if imag[order] is None:
                    parts = (real[order] * cos, -(real[order] * sin))
                else:
                    parts = (
                        real[order] * cos + imag[order] * sin,
                        imag[order] * cos - real[order] * sin,
                    )
                for side, part in enumerate(parts):
                    spot = (pl.ds(16 * order, 16), pl.ds(WIDE * side + 128 * tile, 128))
                    high = part.astype(jnp.bfloat16)
                    z_hi[spot] = high
                    z_lo[spot] = (part - high.astype(jnp.float32)).astype(jnp.bfloat16)

        def product(index):
            high, low = z_hi[...], z_lo[...]
            return (
                jnp.dot(high, mat_ref[index], preferred_element_type=jnp.float32)
                + jnp.dot(low, mat_ref[index], preferred_element_type=jnp.float32)
                + jnp.dot(high, mat_ref[index + 1], preferred_element_type=jnp.float32)
            )

        damping = gain[...].reshape(16 * WAVES, WIDE)
        waves = product(0) * jnp.concatenate([damping, damping], axis=1)
        high = waves.astype(jnp.bfloat16)
        z_hi[...] = high
        z_lo[...] = (waves - high.astype(jnp.float32)).astype(jnp.bfloat16)
        spread[...] = product(2)
        for tile in range(2):
            real, imag = [], []
            for order in range(WAVES):
                rows = pl.ds(16 * order, 16)
                lanes = pl.ds(128 * tile, 128)
                cos = jnp.broadcast_to(tab_ref[0, order : order + 1, lanes], (16, 128))
                sin = jnp.broadcast_to(tab_ref[1, order : order + 1, lanes], (16, 128))
                re = spread[rows, lanes]
                im = spread[rows, pl.ds(WIDE + 128 * tile, 128)]
                real.append(re * cos - im * sin)
                imag.append(im * cos + re * sin)
            for block, value in enumerate(backward_blocks(real, imag)):
                sent[1 + item, block, :, pl.ds(128 * tile, 128)] = value
        start_turn(1 + item)

    level = lax.broadcasted_iota(jnp.int32, (16, 128), 0)
    running = share_ref[0]
    share = jnp.full((16, 128), share_ref[0])
    top_share = share
    for target in range(1, 16):
        running = running + share_ref[target]
        share = jnp.where(level >= target, share_ref[target], share)
        top_share = jnp.where(level >= target, running, top_share)
    whole = jnp.full((16, 128), running)
    share = share / whole
    top_share = top_share / whole

    for item in range(4):
        for step in range(1, GROUPS):
            source = lax.rem(group + GROUPS - step, GROUPS)
            pltpu.make_async_remote_copy(
                src_ref=sent.at[item, pl.ds(0, PER)],
                dst_ref=held.at[item, source],
                send_sem=turn_send.at[item, step - 1],
                recv_sem=turn_recv.at[item, step - 1],
                device_id=(band, source),
                device_id_type=MESH,
            ).wait_recv()
        keep(item).wait()

    def remap(step, carry):
        block = step // 2
        lanes = pl.ds(pl.multiple_of(128 * lax.rem(step, 2), 128), 128)
        place = pl.ds(pl.multiple_of(128 * step, 128), 128)
        for row in range(ROWS):
            def source(item, index):
                at = LEVELS * row + index % LEVELS
                line = held[item, index // LEVELS, block, pl.ds(at, 1), lanes]
                return line

            total = source(0, 0)
            for index in range(1, 16):
                total = total + source(0, index)
            total = jnp.broadcast_to(total, (16, 128))
            target = total * share
            top = total * top_share
            bottom = top - target
            lower = jnp.zeros((1, 128), jnp.float32)
            sums = [jnp.zeros((16, 128), jnp.float32)] * 3
            for index in range(16):
                upper = lower + source(0, index)
                common = jnp.maximum(
                    jnp.minimum(top, jnp.broadcast_to(upper, (16, 128)))
                    - jnp.maximum(bottom, jnp.broadcast_to(lower, (16, 128))),
                    0.0,
                )
                sums = [
                    one + common * jnp.broadcast_to(source(1 + item, index), (16, 128))
                    for item, one in enumerate(sums)
                ]
                lower = upper
            inverse = 1.0 / target
            spread_out = [sums[2] * inverse, sums[1] * inverse, sums[0] * inverse, target]
            for item in range(4):
                field_out[item, row, :, place] = spread_out[item]
        return carry

    lax.fori_loop(0, 2 * PER, remap, 0)

    lane = lax.broadcasted_iota(jnp.int32, (16, PER * WIDE), 1)

    def pack(step, carry):
        item, row = step // ROWS, lax.rem(step, ROWS)
        wide = field_out[item, row]
        packed = pltpu.roll(wide, PER * WIDE - EDGE, 1)
        for block in range(1, PER):
            shift = EDGE + (WIDE - FINE) * block
            packed = jnp.where(
                lane >= FINE * block, pltpu.roll(wide, PER * WIDE - shift, 1), packed
            )
        out_ref[item, row] = packed[:, : LON // GROUPS]
        return carry

    lax.fori_loop(0, 4 * ROWS, pack, 0)

    for copy in halos:
        copy.wait_send()
    for item in range(4):
        for step in range(1, GROUPS):
            turn(item, step).wait_send()


def on_device(
    zonal_velocity, meridional_velocity, heat_anomaly, layer_pressure_depth, reference_layer_shares
):
    matrices, tables = constants()
    f32 = jnp.float32
    vmem = pl.BlockSpec(memory_space=pltpu.VMEM)
    smem = pl.BlockSpec(memory_space=pltpu.SMEM)
    size = 16 * WAVES
    result = pl.pallas_call(
        kernel,
        out_shape=jax.ShapeDtypeStruct((4, ROWS, 16, LON // GROUPS), f32),
        in_specs=[smem, smem] + [vmem] * 6,
        out_specs=vmem,
        scratch_shapes=[
            pltpu.VMEM((2, 8, 8, 2944), f32),
            pltpu.VMEM((2, 8, COARSE, 8, WIDE), f32),
            pltpu.VMEM((3, COARSE, 16, WIDE), f32),
            pltpu.VMEM((4, COARSE, 16, WIDE), f32),
            pltpu.VMEM((4, GROUPS, PER, 16, WIDE), f32),
            pltpu.VMEM((size, 2 * WIDE), f32),
            pltpu.VMEM((WAVES, 16, WIDE), f32),
            pltpu.VMEM((size, 2 * WIDE), jnp.bfloat16),
            pltpu.VMEM((size, 2 * WIDE), jnp.bfloat16),
            pltpu.VMEM((4, ROWS, 16, PER * WIDE), f32),
            pltpu.SemaphoreType.DMA((2, 2)),
            pltpu.SemaphoreType.DMA((2, 2)),
            pltpu.SemaphoreType.DMA((4, 3)),
            pltpu.SemaphoreType.DMA((4, 3)),
            pltpu.SemaphoreType.DMA((4,)),
        ],
        compiler_params=pltpu.CompilerParams(
            collective_id=0, has_side_effects=True, vmem_limit_bytes=40 << 20
        ),
        cost_estimate=pl.CostEstimate(
            flops=2_000_000_000, bytes_accessed=4_000_000, transcendentals=0
        ),
    )(
        jnp.asarray(grid_table(lax.axis_size("lat"))),
        reference_layer_shares,
        zonal_velocity,
        meridional_velocity,
        heat_anomaly,
        layer_pressure_depth,
        jnp.asarray(matrices),
        jnp.asarray(tables),
    )
    result = jnp.transpose(result, (0, 2, 1, 3))
    return (result[0], result[1], result[2], result[3])


def solution(mesh):
    return jax.shard_map(
        on_device,
        mesh=mesh,
        in_specs=(
            P("lev", "lat", None),
            P("lev", "lat", None),
            P("lev", "lat", None),
            P("lev", "lat", None),
            P(),
        ),
        out_specs=(
            P(None, "lat", "lev"),
            P(None, "lat", "lev"),
            P(None, "lat", "lev"),
            P(None, "lat", "lev"),
        ),
        check_vma=False,
    )
```

profile of v0, /device:TPU:1, one launch (start us, length us, event | category | flops | bytes accessed | tf_op | source)
XLA Modules:
  0.0 52.3 jit_solution(17726417887525763817)
XLA Ops:
  0.6 0.0 copy-start
  0.6 0.9 %copy-done = f32[4,4,2880]{2,1,0:T(4,128)S(1)} copy-done((f32[4,4,2880]{2,1,0:T(4,128)S(1)}, f32[4,4,2880]{2,1,0:T(4,128)}, u32[]{:S(2)}) %copy-start) | copy-done | bytes 184344
  1.6 0.0 copy-start.1
  1.6 0.9 %copy-done.1 = f32[4,4,2880]{2,1,0:T(4,128)S(1)} copy-done((f32[4,4,2880]{2,1,0:T(4,128)S(1)}, f32[4,4,2880]{2,1,0:T(4,128)}, u32[]{:S(2)}) %copy-start.1) | copy-done | bytes 184344
  2.5 0.0 copy-start.2
  2.5 0.9 %copy-done.2 = f32[4,4,2880]{2,1,0:T(4,128)S(1)} copy-done((f32[4,4,2880]{2,1,0:T(4,128)S(1)}, f32[4,4,2880]{2,1,0:T(4,128)}, u32[]{:S(2)}) %copy-start.2) | copy-done | bytes 184344
  3.4 0.0 copy-start.3
  3.4 0.9 %copy-done.3 = f32[4,4,2880]{2,1,0:T(4,128)S(1)} copy-done((f32[4,4,2880]{2,1,0:T(4,128)S(1)}, f32[4,4,2880]{2,1,0:T(4,128)}, u32[]{:S(2)}) %copy-start.3) | copy-done | bytes 184344
  4.3 0.0 copy-start.4
  4.3 0.7 %copy-done.4 = f32[16]{0:T(128)S(1)} copy-done((f32[16]{0:T(128)S(1)}, f32[16]{0:T(128)}, u32[]{:S(2)}) %copy-start.4) | copy-done | bytes 88
  5.0 0.0 copy-start.5
  5.0 1.6 %copy-done.5 = bf16[4,512,512]{2,1,0:T(8,128)(2,1)S(1)} copy-done((bf16[4,512,512]{2,1,0:T(8,128)(2,1)S(1)}, bf16[4,512,512]{2,1,0:T(8,128)(2,1)}, u32[]{:S(2)}) %copy-start.5) | copy-done | bytes 2097176
  6.6 0.0 copy-start.6
  6.6 0.8 %copy-done.6 = f32[64,16]{1,0:T(8,128)S(1)} copy-done((f32[64,16]{1,0:T(8,128)S(1)}, f32[64,16]{1,0:T(8,128)}, u32[]{:S(2)}) %copy-start.6) | copy-done | bytes 4120
  7.3 0.0 copy-start.7
  7.3 0.7 %copy-done.7 = f32[3,8,256]{2,1,0:T(8,128)S(1)} copy-done((f32[3,8,256]{2,1,0:T(8,128)S(1)}, f32[3,8,256]{2,1,0:T(8,128)}, u32[]{:S(2)}) %copy-start.7) | copy-done | bytes 24600
  8.1 41.0 %shard_map.111 = f32[4,4,16,720]{3,2,1,0:T(8,128)S(1)} custom-call(f32[64,16]{1,0:T(8,128)S(1)} %copy-done.6, f32[16]{0:T(128)S(1)} %copy-done.4, f32[4,4,2880]{2,1,0:T(4,128)S(1)} %copy-done, f32[4,4,2880]{2,1,0:T(4,128)S(1)} %copy-done.1, f32[4,4,2880]{2,1,0:T(4,128)S(1)} %copy-done.2, f32[4,4,2880]{2,1,0:T(4,128)S(1)} %copy-done.3, ...), custom_call_target="tpu_custom_call" | custom-call | flops 2000000000 | bytes 4000000 | tf_op jit(solution)/shard_map/pallas_call | solution.py:465
  49.1 0.1 slice_bitcast_fusion
  49.1 0.8 %copy.15 = f32[16,4,720]{2,1,0:T(4,128)} copy(f32[16,4,720]{2,0,1:T(8,128)S(1)} %get-tuple-element.8) | data formatting | bytes 368640
  49.9 0.8 %copy.14 = f32[16,4,720]{2,1,0:T(4,128)} copy(f32[16,4,720]{2,0,1:T(8,128)S(1)} %get-tuple-element.9) | data formatting | bytes 368640
  50.7 0.8 %copy.13 = f32[16,4,720]{2,1,0:T(4,128)} copy(f32[16,4,720]{2,0,1:T(8,128)S(1)} %get-tuple-element.10) | data formatting | bytes 368640
  51.5 0.8 %copy.12 = f32[16,4,720]{2,1,0:T(4,128)} copy(f32[16,4,720]{2,0,1:T(8,128)S(1)} %get-tuple-element.11) | data formatting | bytes 368640
Async XLA Ops:
  0.6 0.9 %copy-start = (f32[4,4,2880]{2,1,0:T(4,128)S(1)}, f32[4,4,2880]{2,1,0:T(4,128)}, u32[]{:S(2)}) copy-start(f32[4,4,2880]{2,1,0:T(4,128)} %u_ref.1) | copy-start | bytes 552964
  1.6 0.9 %copy-start.1 = (f32[4,4,2880]{2,1,0:T(4,128)S(1)}, f32[4,4,2880]{2,1,0:T(4,128)}, u32[]{:S(2)}) copy-start(f32[4,4,2880]{2,1,0:T(4,128)} %v_ref.1) | copy-start | bytes 552964
  2.5 0.9 %copy-start.2 = (f32[4,4,2880]{2,1,0:T(4,128)S(1)}, f32[4,4,2880]{2,1,0:T(4,128)}, u32[]{:S(2)}) copy-start(f32[4,4,2880]{2,1,0:T(4,128)} %t_ref.1) | copy-start | bytes 552964
  3.4 0.9 %copy-start.3 = (f32[4,4,2880]{2,1,0:T(4,128)S(1)}, f32[4,4,2880]{2,1,0:T(4,128)}, u32[]{:S(2)}) copy-start(f32[4,4,2880]{2,1,0:T(4,128)} %h_ref.1) | copy-start | bytes 552964
  4.3 0.7 %copy-start.4 = (f32[16]{0:T(128)S(1)}, f32[16]{0:T(128)}, u32[]{:S(2)}) copy-start(f32[16]{0:T(128)} %share_ref.1) | copy-start | bytes 196
  5.0 1.6 %copy-start.5 = (bf16[4,512,512]{2,1,0:T(8,128)(2,1)S(1)}, bf16[4,512,512]{2,1,0:T(8,128)(2,1)}, u32[]{:S(2)}) copy-start(bf16[4,512,512]{2,1,0:T(8,128)(2,1)} %constant.7.clone.mat_ref) | copy-start | bytes 6291460
  6.6 0.8 %copy-start.6 = (f32[64,16]{1,0:T(8,128)S(1)}, f32[64,16]{1,0:T(8,128)}, u32[]{:S(2)}) copy-start(f32[64,16]{1,0:T(8,128)} %constant.6.clone.grid_ref) | copy-start | bytes 12292
  7.3 0.7 %copy-start.7 = (f32[3,8,256]{2,1,0:T(8,128)S(1)}, f32[3,8,256]{2,1,0:T(8,128)}, u32[]{:S(2)}) copy-start(f32[3,8,256]{2,1,0:T(8,128)} %constant.8.clone.tab_ref) | copy-start | bytes 73732
where the time goes:
time: 52.7 us; the launch traced here: 52.3 us
  Pallas kernels  41 us (78%)
  local copies, waits for them, and re-layouts  10.7 us (20%)
  between operations  0.67 us (1%)
    pallas_call x1, Pallas kernels, on_device(): pl.pallas_call(kernel, out_shape=jax.ShapeDtypeStruct((4, ROWS, 16, LON /...  41 us
    unnamed x20, local copies, waits for them, and re-layouts  10.6 us

commit v1 on v0

v1 whole, which is shorter than its diff:
```python
import math

import jax
import jax.numpy as jnp
import numpy as np
from jax import lax
from jax.experimental import pallas as pl
from jax.experimental.pallas import tpu as pltpu
from jax.sharding import PartitionSpec as P

SPEED = 0.04
QUARTER = math.cos(math.pi / 4.0)
SPACING = 180.0 / 1440.0
LON = 2880
ROWS = 4
LEVELS = 4
GROUPS = 4
COARSE = 12
FINE = 240
WIDE = 256
EDGE = 8
PER = COARSE // GROUPS
WAVES = COARSE // 2 + 1
MESH = pl.DeviceIdType.MESH


def grid_table(bands):
    f32 = np.float32
    rows = np.arange(bands * ROWS)
    faces = np.arange(bands * ROWS + 1)
    scale = f32(math.pi / 180.0)
    center = np.cos(((rows.astype(f32) + f32(0.5)) * f32(SPACING) - f32(90.0)) * scale)
    face = np.cos((faces.astype(f32) * f32(SPACING) - f32(90.0)) * scale)
    face = np.where(faces == 0, f32(0.0), face)
    table = np.zeros((bands, 4, 8, 128), f32)
    for sub in range(8):
        row = ROWS * np.arange(bands) + sub % ROWS
        table[:, 0, sub] = (f32(1.0) / center[row])[:, None]
        table[:, 1, sub] = face[row + 1][:, None]
        outer = ROWS * np.arange(bands) + (0 if sub % ROWS < 2 else ROWS)
        table[:, 2, sub] = face[outer][:, None]
        table[:, 3, sub] = (center[row] / f32(QUARTER))[:, None]
    return table


def split_bf16(array):
    high = array.astype(jnp.bfloat16)
    low = (array - high.astype(np.float32)).astype(jnp.bfloat16)
    return high, low


def constants():
    cell = np.arange(FINE)
    wave = np.arange(FINE)
    angle = 2.0 * np.pi * (np.outer(cell, wave) % FINE) / FINE
    cos, sin = np.cos(angle), np.sin(angle)
    forward = np.zeros((2 * WIDE, 2 * WIDE))
    spots = slice(EDGE, EDGE + FINE)
    spots_im = slice(WIDE + EDGE, WIDE + EDGE + FINE)
    forward[spots, 0:FINE] = cos
    forward[spots, WIDE : WIDE + FINE] = -sin
    forward[spots_im, 0:FINE] = sin
    forward[spots_im, WIDE : WIDE + FINE] = cos
    backward = np.zeros((2 * WIDE, 2 * WIDE))
    backward[0:FINE, spots] = cos.T
    backward[0:FINE, spots_im] = sin.T
    backward[WIDE : WIDE + FINE, spots] = -sin.T
    backward[WIDE : WIDE + FINE, spots_im] = cos.T
    matrices = np.stack(
        [m for whole in (forward, backward) for m in split_bf16(whole.astype(np.float32))]
    )
    tables = np.zeros((3, 8, WIDE), np.float32)
    for order in range(WAVES):
        turn = 2.0 * np.pi * order * cell / LON
        tables[0, order, spots] = np.cos(turn)
        tables[1, order, spots] = np.sin(turn)
        number = (order + COARSE * wave).astype(np.float32)
        tables[2, order, 0:FINE] = np.sin(number * np.float32(math.pi / LON))
    return matrices, tables


def cos_of(index):
    value = math.cos(2.0 * math.pi * index / COARSE)
    return round(value) if abs(value - round(value)) < 1e-9 else round(2 * value) / 2 if abs(
        2 * value - round(2 * value)
    ) < 1e-9 else value


def combine(terms):
    total = None
    for factor, array in terms:
        if factor == 0:
            continue
        if total is None:
            total = array if factor == 1 else -array if factor == -1 else factor * array
        elif factor == 1:
            total = total + array
        elif factor == -1:
            total = total - array
        else:
            total = total + factor * array
    return total


def forward_blocks(x):
    even = {n: x[n] + x[COARSE - n] for n in range(1, 6)}
    odd = {n: x[n] - x[COARSE - n] for n in range(1, 6)}
    ends = {0: x[0] + x[6], 1: x[0] - x[6]}
    even_sum = {n: even[n] + even[6 - n] for n in (1, 2)}
    even_dif = {n: even[n] - even[6 - n] for n in (1, 2)}
    odd_sum = {n: odd[n] + odd[6 - n] for n in (1, 2)}
    odd_dif = {n: odd[n] - odd[6 - n] for n in (1, 2)}
    real, imag = [], []
    for k in range(WAVES):
        pick = even_dif if k % 2 else even_sum
        terms = [(1, ends[k % 2])] + [(cos_of(n * k), pick[n]) for n in (1, 2)]
        terms.append((cos_of(3 * k), even[3]))
        real.append(combine(terms))
        if 0 < k < 6:
            pick = odd_sum if k % 2 else odd_dif
            terms = [(-cos_of(n * k - 3), pick[n]) for n in (1, 2)]
            terms.append((-cos_of(3 * k - 3), odd[3]))
            imag.append(combine(terms))
        else:
            imag.append(None)
    return real, imag


def backward_blocks(real, imag):
    base = {0: real[0] + real[6], 1: real[0] - real[6]}
    blocks = [None] * COARSE
    for b in range(0, 7):
        cosine = combine([(1, base[b % 2])] + [(cos_of(k * b), real[k]) for k in range(1, 6)])
        if b in (0, 6):
            blocks[b] = cosine
            continue
        sine = combine([(-cos_of(k * b - 3), imag[k]) for k in range(1, 6)])
        blocks[b] = cosine + sine
        blocks[COARSE - b] = cosine - sine
    return blocks


def minmod(left, right):
    return jnp.maximum(jnp.minimum(left, right), 0.0) + jnp.minimum(jnp.maximum(left, right), 0.0)


def window(load, block):
    lane = lax.broadcasted_iota(jnp.int32, (8, WIDE), 1)
    if block == 0:
        body = pltpu.roll(load(0, 256), EDGE, 1)
        tail = pltpu.roll(load(2816, LON), 128 - (LON - EDGE - 2816), 1)
        return jnp.concatenate(
            [jnp.where(lane[:, :128] < EDGE, tail, body[:, :128]), body[:, 128:]], axis=1
        )
    start = FINE * block - EDGE
    first = start // 128 * 128
    body = pltpu.roll(load(first, first + 384), (384 - (start - first)) % 384, 1)[:, :WIDE]
    if block == COARSE - 1:
        head = pltpu.roll(load(0, 256), WIDE - EDGE, 1)
        body = jnp.where(lane >= WIDE - EDGE, head, body)
    return body


def limits(courant):
    return jnp.where(courant >= 0.0, 0.5, -0.5) - 0.5 * courant


def kernel(
    grid_hbm, share_hbm, u_hbm, v_hbm, t_hbm, h_hbm, mat_hbm, tab_hbm,
    out_ref,
    given, mat_ref, tab_ref, grid_ref, share_ref,
    own, to_up, to_down, from_down, from_up, base, lean_ref, inverse_h,
    field, sent, held, spread, gain, z_hi, z_lo, weight, wide, target_ref,
    in_sem, halo_send, halo_recv, turn_send, turn_recv, own_sem,
):
    bands = lax.axis_size("lat")
    band = lax.axis_index("lat")
    group = lax.axis_index("lev")
    above = (lax.rem(band + 1, bands), group)
    below = (lax.rem(band + bands - 1, bands), group)
    partners = [(band, lax.rem(group + step, GROUPS)) for step in range(1, GROUPS)]

    barrier = pltpu.get_barrier_semaphore()
    for device in [above, below] + partners:
        pl.semaphore_signal(barrier, inc=1, device_id=device, device_id_type=MESH)

    loads = [
        pltpu.make_async_copy(source, given.at[item], in_sem.at[item])
        for item, source in enumerate((h_hbm, v_hbm, u_hbm, t_hbm))
    ]
    tables = [
        pltpu.make_async_copy(grid_hbm.at[band], grid_ref, in_sem.at[4]),
        pltpu.make_async_copy(tab_hbm, tab_ref, in_sem.at[5]),
        pltpu.make_async_copy(share_hbm, share_ref, in_sem.at[6]),
        pltpu.make_async_copy(mat_hbm, mat_ref, in_sem.at[7]),
    ]
    for copy in loads + tables:
        copy.start()

    def sub_row(shape):
        return lax.rem(lax.broadcasted_iota(jnp.int32, shape, 0), ROWS)

    place = sub_row((8, WIDE))

    def down(array, step):
        return pltpu.roll(array, step % 8, 0)

    def side(array, step):
        return pltpu.roll(array, step % WIDE, 1)

    def cut_item(item):
        for pair in range(2):

            def load(first, last):
                value = given[item, 2 * pair : 2 * pair + 2, :, first : min(last, LON)]
                value = value.reshape(8, min(last, LON) - first)
                short = -value.shape[1] % 128
                if short:
                    value = jnp.concatenate([value, jnp.zeros((8, short), jnp.float32)], axis=1)
                return value

            for block in range(COARSE):
                own[item, block, pair] = window(load, block)

        def edges(block, carry):
            a, b = own[item, block, 0], own[item, block, 1]
            to_up[item, block] = jnp.where(
                place < 2,
                jnp.where(place == 0, down(a, -3), down(b, -2)),
                jnp.where(place == 2, a, down(b, 1)),
            )
            to_down[item, block] = jnp.where(
                place < 2,
                jnp.where(place == 0, down(b, -1), a),
                jnp.where(place == 2, down(b, 2), down(a, 3)),
            )
            return carry

        lax.fori_loop(0, COARSE, edges, 0)

    def halo(item, way):
        return pltpu.make_async_remote_copy(
            src_ref=(to_down if way else to_up).at[item],
            dst_ref=(from_up if way else from_down).at[item],
            send_sem=halo_send.at[item, way],
            recv_sem=halo_recv.at[item, way],
            device_id=below if way else above,
            device_id_type=MESH,
        )

    halos = [halo(item, way) for item in range(4) for way in range(2)]
    for item in range(4):
        loads[item].wait()
        cut_item(item)
        if item == 0:
            pl.semaphore_wait(barrier, 2 + len(partners))
        for way in range(2):
            halo(item, way).start()
    for copy in tables:
        copy.wait()

    def zonal(block, carry):
        for pair in range(2):
            wind = own[2, block, pair]
            thick = own[0, block, pair]
            c = SPEED * (wind + side(wind, -1))
            up = c >= 0.0
            part = limits(c)
            for item in range(4):
                q = thick if item == 0 else thick * own[item, block, pair]
                after = side(q, -1)
                step = after - q
                tilt = minmod(side(step, 1), step)
                through = c * (
                    jnp.where(up, q, after) + part * jnp.where(up, tilt, side(tilt, -1))
                )
                base[item, block, pair] = q - (through - side(through, 1))
        return carry

    lax.fori_loop(0, COARSE, zonal, 0)

    ratio = jnp.concatenate([grid_ref[3], grid_ref[3]], axis=1)
    for order in range(WAVES):
        sine = jnp.broadcast_to(tab_ref[2, order : order + 1, :], (8, WIDE))
        damping = ratio / jnp.maximum(sine, ratio)
        damping = damping * damping * ((1.0 if order in (0, 6) else 2.0) / LON)
        gain[16 * order : 16 * order + 8] = damping
        gain[16 * order + 8 : 16 * order + 16] = damping

    has_below = jnp.where(band > 0, 1.0, 0.0)
    has_above = jnp.where(band < bands - 1, 1.0, 0.0)

    def outer(a, b):
        return jnp.where(
            place == 1, down(b, 1), jnp.where(place == 2, down(b, -1), a)
        )

    def wide_grid(index):
        return jnp.concatenate([grid_ref[index], grid_ref[index]], axis=1)

    def slants(block, carry):
        a, b = own[1, block, 0], own[1, block, 1]
        near = jnp.where(place < 2, from_down[1, block] * has_below, from_up[1, block] * has_above)
        winds = (a + down(a, -1), b + down(b, -1), near + outer(a, b))
        for index, wind in enumerate(winds):
            c = SPEED * wind
            lean_ref[block, 2 * index] = c * wide_grid(2 if index == 2 else 1)
            lean_ref[block, 2 * index + 1] = limits(c)
        return carry

    def meridional(item):
        def one(block, carry):
            sign = jnp.where(place < 2, 1.0, -1.0)
            low, high = from_down[0, block] * has_below, from_up[0, block] * has_above
            cells = [own[0, block, 0], own[0, block, 1]]
            if item:
                low, high = low * from_down[item, block], high * from_up[item, block]
                cells = [cells[pair] * own[item, block, pair] for pair in range(2)]
            near = jnp.where(place < 2, low, high)
            far = jnp.where(place < 2, down(low, -2), down(high, 2))
            edge = outer(*cells)
            gap = edge - near
            near_slope = sign * minmod(near - far, gap)
            gap = sign * gap
            slopes, flows = [], []
            for pair in range(2):
                x = cells[pair]
                after = down(x, -1)
                inner = after - x
                upper = jnp.where(place == 3, down(gap, 1) if pair else gap, inner)
                lower = jnp.where(place == 0, down(gap, -1) if pair else gap, down(inner, 1))
                slope = minmod(lower, upper)
                slopes.append(slope)
                part = lean_ref[block, 2 * pair + 1]
                up = part > 0.0
                flows.append(
                    lean_ref[block, 2 * pair]
                    * (jnp.where(up, x, after) + part * jnp.where(up, slope, down(slope, -1)))
                )
            part = lean_ref[block, 5]
            pick = part * sign > 0.0
            flow = lean_ref[block, 4] * (
                jnp.where(pick, near, edge) + part * jnp.where(pick, near_slope, outer(*slopes))
            )
            for pair in range(2):
                above_flow = jnp.where(place == 3, down(flow, 1) if pair else flow, flows[pair])
                below_flow = jnp.where(
                    place == 0, down(flow, -1) if pair else flow, down(flows[pair], 1)
                )
                value = base[item, block, pair] - (above_flow - below_flow) * wide_grid(0)
                rows = pl.ds(8 * pair, 8)
                if item == 0:
                    sent[0, block, rows] = value
                    inverse_h[block, rows] = 1.0 / value
                else:
                    field[block, rows] = value * inverse_h[block, rows]
            return carry

        lax.fori_loop(0, COARSE, one, 0)

    def turn(item, step):
        target = lax.rem(group + step, GROUPS)
        return pltpu.make_async_remote_copy(
            src_ref=sent.at[item, pl.ds(PER * target, PER)],
            dst_ref=held.at[item, group],
            send_sem=turn_send.at[item, step - 1],
            recv_sem=turn_recv.at[item, step - 1],
            device_id=(band, target),
            device_id_type=MESH,
        )

    def keep(item):
        return pltpu.make_async_copy(
            sent.at[item, pl.ds(PER * group, PER)], held.at[item, group], own_sem.at[item]
        )

    def start_turn(item):
        for step in (2, 3, 1):
            turn(item, step).start()
        keep(item).start()

    def end_turn(item):
        for step in range(1, GROUPS):
            source = lax.rem(group + GROUPS - step, GROUPS)
            pltpu.make_async_remote_copy(
                src_ref=sent.at[item, pl.ds(0, PER)],
                dst_ref=held.at[item, source],
                send_sem=turn_send.at[item, step - 1],
                recv_sem=turn_recv.at[item, step - 1],
                device_id=(band, source),
                device_id_type=MESH,
            ).wait_recv()
        keep(item).wait()

    def product(index):
        high, low = z_hi[...], z_lo[...]
        return (
            jnp.dot(high, mat_ref[index], preferred_element_type=jnp.float32)
            + jnp.dot(low, mat_ref[index], preferred_element_type=jnp.float32)
            + jnp.dot(high, mat_ref[index + 1], preferred_element_type=jnp.float32)
        )

    def polar(item):
        def forward(tile, carry):
            lanes = pl.ds(pl.multiple_of(128 * tile, 128), 128)
            real, imag = forward_blocks([field[block, :, lanes] for block in range(COARSE)])
            for order in range(WAVES):
                cos = jnp.broadcast_to(tab_ref[0, order : order + 1, lanes], (16, 128))
                sin = jnp.broadcast_to(tab_ref[1, order : order + 1, lanes], (16, 128))
                if imag[order] is None:
                    parts = (real[order] * cos, -(real[order] * sin))
                else:
                    parts = (
                        real[order] * cos + imag[order] * sin,
                        imag[order] * cos - real[order] * sin,
                    )
                for half, part in enumerate(parts):
                    at = pl.multiple_of(WIDE * half + 128 * tile, 128)
                    spot = (pl.ds(16 * order, 16), pl.ds(at, 128))
                    high = part.astype(jnp.bfloat16)
                    z_hi[spot] = high
                    z_lo[spot] = (part - high.astype(jnp.float32)).astype(jnp.bfloat16)
            return carry

        lax.fori_loop(0, 2, forward, 0)
        damping = gain[...]
        waves = product(0) * jnp.concatenate([damping, damping], axis=1)
        high = waves.astype(jnp.bfloat16)
        z_hi[...] = high
        z_lo[...] = (waves - high.astype(jnp.float32)).astype(jnp.bfloat16)
        spread[...] = product(2)

        def backward(tile, carry):
            lanes = pl.ds(pl.multiple_of(128 * tile, 128), 128)
            other = pl.ds(pl.multiple_of(WIDE + 128 * tile, 128), 128)
            real, imag = [], []
            for order in range(WAVES):
                rows = pl.ds(16 * order, 16)
                cos = jnp.broadcast_to(tab_ref[0, order : order + 1, lanes], (16, 128))
                sin = jnp.broadcast_to(tab_ref[1, order : order + 1, lanes], (16, 128))
                re, im = spread[rows, lanes], spread[rows, other]
                real.append(re * cos - im * sin)
                imag.append(im * cos + re * sin)
            for block, value in enumerate(backward_blocks(real, imag)):
                sent[item, block, :, lanes] = value
            return carry

        lax.fori_loop(0, 2, backward, 0)

    def end_halo(item):
        for way in range(2):
            halo(item, way).wait_recv()

    end_halo(0)
    end_halo(1)
    lax.fori_loop(0, COARSE, slants, 0)
    meridional(0)
    start_turn(0)
    for item in range(1, 4):
        if item > 1:
            end_halo(item)
        meridional(item)
        polar(item)
        start_turn(item)

    first_half = lax.broadcasted_iota(jnp.int32, (8, 128), 0) < ROWS

    def lines(item, block, lanes):
        found = []
        for index in range(8):
            both = held[item, index // 2, block, pl.ds(8 * (index % 2), 8), lanes]
            turned = down(both, ROWS)
            found.append(jnp.where(first_half, both, turned))
            found.append(jnp.where(first_half, turned, both))
        return found

    def tile_of(step):
        return step // 2, pl.ds(pl.multiple_of(128 * lax.rem(step, 2), 128), 128)

    def weigh(step, carry):
        uppers = []
        for line in lines(0, *tile_of(step)):
            uppers.append(uppers[-1] + line if uppers else line)
        total = uppers[-1]
        lowers = [jnp.zeros((8, 128), jnp.float32)] + uppers[:-1]
        running = share_ref[0]
        for level in range(1, 16):
            running = running + share_ref[level]
        unit = total / jnp.full((8, 128), running)
        running = jnp.float32(0.0)
        for pair in range(8):
            one, two = share_ref[2 * pair], share_ref[2 * pair + 1]
            target = unit * jnp.where(first_half, one, two)
            top = unit * jnp.where(first_half, running + one, running + one + two)
            running = running + one + two
            bottom = top - target
            wide[pair, step] = target
            target_ref[step, pair] = 1.0 / target
            for index in range(16):
                weight[step, pair, index] = jnp.maximum(
                    jnp.minimum(top, uppers[index]) - jnp.maximum(bottom, lowers[index]), 0.0
                )
        return carry

    def gather(item):
        def one(step, carry):
            found = lines(item, *tile_of(step))
            for pair in range(8):
                total = weight[step, pair, 0] * found[0]
                for index in range(1, 16):
                    total = total + weight[step, pair, index] * found[index]
                wide[pair, step] = total * target_ref[step, pair]
            return carry

        lax.fori_loop(0, 2 * PER, one, 0)

    def pack(output):
        def one(pair, carry):
            lane = lax.broadcasted_iota(jnp.int32, (8, 128), 1)
            shifts = (128 - EDGE, 104, 88)
            t = [pltpu.roll(wide[pair, step], shifts[step // 2], 1) for step in range(6)]
            tiles = [
                jnp.where(lane < 120, t[0], t[1]),
                jnp.where(lane < 112, t[1], t[2]),
                jnp.where(lane < 104, t[2], t[3]),
                jnp.where(lane < 96, t[3], t[4]),
                jnp.where(lane < 88, t[4], t[5]),
                t[5],
            ]
            for at, tile in enumerate(tiles):
                size = min(128, LON // GROUPS - 128 * at)
                value = tile[:, :size].reshape(2, ROWS, size)
                out_ref[output, pl.ds(2 * pair, 2), :, 128 * at : 128 * at + size] = value
            return carry

        lax.fori_loop(0, 8, one, 0)

    end_turn(0)
    lax.fori_loop(0, 2 * PER, weigh, 0)
    pack(3)
    for item in range(1, 4):
        end_turn(item)
        gather(item)
        pack((0, 2, 1, 0)[item])

    for copy in halos:
        copy.wait_send()
    for item in range(4):
        for step in range(1, GROUPS):
            turn(item, step).wait_send()


def on_device(
    zonal_velocity, meridional_velocity, heat_anomaly, layer_pressure_depth, reference_layer_shares
):
    matrices, tables = constants()
    f32 = jnp.float32
    hbm = pl.BlockSpec(memory_space=pl.ANY)
    size = 16 * WAVES
    result = pl.pallas_call(
        kernel,
        out_shape=jax.ShapeDtypeStruct((4, 16, ROWS, LON // GROUPS), f32),
        in_specs=[hbm] * 8,
        out_specs=pl.BlockSpec(memory_space=pltpu.VMEM),
        scratch_shapes=[
            pltpu.VMEM((4, LEVELS, ROWS, LON), f32),
            pltpu.VMEM((4, 2 * WIDE, 2 * WIDE), jnp.bfloat16),
            pltpu.VMEM((3, 8, WIDE), f32),
            pltpu.VMEM((4, 8, 128), f32),
            pltpu.SMEM((16,), f32),
            pltpu.VMEM((4, COARSE, 2, 8, WIDE), f32),
            pltpu.VMEM((4, COARSE, 8, WIDE), f32),
            pltpu.VMEM((4, COARSE, 8, WIDE), f32),
            pltpu.VMEM((4, COARSE, 8, WIDE), f32),
            pltpu.VMEM((4, COARSE, 8, WIDE), f32),
            pltpu.VMEM((4, COARSE, 2, 8, WIDE), f32),
            pltpu.VMEM((COARSE, 6, 8, WIDE), f32),
            pltpu.VMEM((COARSE, 16, WIDE), f32),
            pltpu.VMEM((COARSE, 16, WIDE), f32),
            pltpu.VMEM((4, COARSE, 16, WIDE), f32),
            pltpu.VMEM((4, GROUPS, PER, 16, WIDE), f32),
            pltpu.VMEM((size, 2 * WIDE), f32),
            pltpu.VMEM((size, WIDE), f32),
            pltpu.VMEM((size, 2 * WIDE), jnp.bfloat16),
            pltpu.VMEM((size, 2 * WIDE), jnp.bfloat16),
            pltpu.VMEM((2 * PER, 8, 16, 8, 128), f32),
            pltpu.VMEM((8, 2 * PER, 8, 128), f32),
            pltpu.VMEM((2 * PER, 8, 8, 128), f32),
            pltpu.SemaphoreType.DMA((8,)),
            pltpu.SemaphoreType.DMA((4, 2)),
            pltpu.SemaphoreType.DMA((4, 2)),
            pltpu.SemaphoreType.DMA((4, 3)),
            pltpu.SemaphoreType.DMA((4, 3)),
            pltpu.SemaphoreType.DMA((4,)),
        ],
        compiler_params=pltpu.CompilerParams(
            collective_id=0, has_side_effects=True, vmem_limit_bytes=56 << 20
        ),
        cost_estimate=pl.CostEstimate(
            flops=2_000_000_000, bytes_accessed=4_000_000, transcendentals=0
        ),
    )(
        jnp.asarray(grid_table(lax.axis_size("lat"))),
        reference_layer_shares,
        zonal_velocity,
        meridional_velocity,
        heat_anomaly,
        layer_pressure_depth,
        jnp.asarray(matrices),
        jnp.asarray(tables),
    )
    return (result[0], result[1], result[2], result[3])


def solution(mesh):
    return jax.shard_map(
        on_device,
        mesh=mesh,
        in_specs=(
            P("lev", "lat", None),
            P("lev", "lat", None),
            P("lev", "lat", None),
            P("lev", "lat", None),
            P(),
        ),
        out_specs=(
            P(None, "lat", "lev"),
            P(None, "lat", "lev"),
            P(None, "lat", "lev"),
            P(None, "lat", "lev"),
        ),
        check_vma=False,
    )
```

time: 52.7 us -> 35.8 us (0.68)
  local copies, waits for them, and re-layouts: 10.7 us -> 2.11 us
  Pallas kernels: 41 us -> 32.9 us
    unnamed x20 -> x0, local copies, waits for them, and re-layouts: 10.6 us -> none
    pallas_call x1, Pallas kernels: 41 us -> 32.9 us  [on_device(): pl.pallas_call(kernel, out_shape=jax.ShapeDtypeStruct((4, 16, ROWS, LON /...]
    squeeze x1, local copies, waits for them, and re-layouts: 0.05 us -> 2.11 us  [on_device(): return (result[0], result[1], result[2], result[3])]
where the time goes in v1:
time: 35.8 us; the launch traced here: 35.6 us
  Pallas kernels  32.9 us (92%)
  local copies, waits for them, and re-layouts  2.11 us (6%)
  between operations  0.64 us (2%)
    pallas_call x1, Pallas kernels, on_device(): pl.pallas_call(kernel, out_shape=jax.ShapeDtypeStruct((4, 16, ROWS, LON /...  32.9 us
    squeeze x1, local copies, waits for them, and re-layouts, on_device(): return (result[0], result[1], result[2], result[3])  2.11 us

profile of v1, /device:TPU:1, one launch (start us, length us, event | category | flops | bytes accessed | tf_op | source)
XLA Modules:
  0.0 35.6 jit_solution(14144267985093661963)
XLA Ops:
  0.6 32.9 %shard_map.111 = f32[4,16,4,720]{3,2,1,0:T(4,128)} custom-call(f32[64,4,8,128]{3,2,1,0:T(8,128)} %constant.6.clone.grid_hbm, f32[16]{0:T(128)} %share_hbm.1, f32[4,4,2880]{2,1,0:T(4,128)} %u_hbm.1, f32[4,4,2880]{2,1,0:T(4,128)} %v_hbm.1, f32[4,4,2880]{2,1,0:T(4,128)} %t_hbm.1, f32[4,4,2880]{2,1,0:T(4,128)} %h_hbm.1, ...), custom_call_target="tpu_custom_call" | custom-call | flops 2000000000 | bytes 4000000 | tf_op jit(solution)/shard_map/pallas_call | solution.py:560
  33.5 2.1 %slice_bitcast_fusion = (f32[16,4,720]{2,1,0:T(4,128)}, f32[16,4,720]{2,1,0:T(4,128)}, f32[16,4,720]{2,1,0:T(4,128)}, f32[16,4,720]{2,1,0:T(4,128)}) fusion(f32[4,16,4,720]{3,2,1,0:T(4,128)} %shard_map.111), kind=kLoop, calls=%fused_computation | loop fusion | bytes 1474560 | tf_op jit(solution)/shard_map/squeeze | solution.py:612

commit v2 on v1

--- a/solution.py
+++ b/solution.py
@@ -180,9 +180,16 @@
     below = (lax.rem(band + bands - 1, bands), group)
     partners = [(band, lax.rem(group + step, GROUPS)) for step in range(1, GROUPS)]
 
+    has_below, has_above = band > 0, band < bands - 1
     barrier = pltpu.get_barrier_semaphore()
-    for device in [above, below] + partners:
+
+    def greet(device):
         pl.semaphore_signal(barrier, inc=1, device_id=device, device_id_type=MESH)
+
+    for device in partners:
+        greet(device)
+    pl.when(has_below)(lambda: greet(below))
+    pl.when(has_above)(lambda: greet(above))
 
     loads = [
         pltpu.make_async_copy(source, given.at[item], in_sem.at[item])
@@ -196,6 +203,14 @@
     ]
     for copy in loads + tables:
         copy.start()
+
+    @pl.when(jnp.logical_not(has_below))
+    def _():
+        from_down[...] = jnp.zeros_like(from_down)
+
+    @pl.when(jnp.logical_not(has_above))
+    def _():
+        from_up[...] = jnp.zeros_like(from_up)
 
     def sub_row(shape):
         return lax.rem(lax.broadcasted_iota(jnp.int32, shape, 0), ROWS)
@@ -248,14 +263,24 @@
             device_id_type=MESH,
         )
 
-    halos = [halo(item, way) for item in range(4) for way in range(2)]
+    def start_halo(item):
+        pl.when(has_above)(lambda: halo(item, 0).start())
+        pl.when(has_below)(lambda: halo(item, 1).start())
+
+    def drain_halo(item):
+        pl.when(has_above)(lambda: halo(item, 0).wait_send())
+        pl.when(has_below)(lambda: halo(item, 1).wait_send())
+
     for item in range(4):
         loads[item].wait()
         cut_item(item)
         if item == 0:
-            pl.semaphore_wait(barrier, 2 + len(partners))
-        for way in range(2):
-            halo(item, way).start()
+            pl.semaphore_wait(
+                barrier,
+                len(partners) + jnp.where(has_below, 1, 0) + jnp.where(has_above, 1, 0),
+            )
+        if item < 2:
+            start_halo(item)
     for copy in tables:
         copy.wait()
 
@@ -268,16 +293,14 @@
             part = limits(c)
             for item in range(4):
                 q = thick if item == 0 else thick * own[item, block, pair]
-                after = side(q, -1)
+                before, after, later = side(q, 1), side(q, -1), side(q, -2)
                 step = after - q
-                tilt = minmod(side(step, 1), step)
-                through = c * (
-                    jnp.where(up, q, after) + part * jnp.where(up, tilt, side(tilt, -1))
-                )
+                first = jnp.where(up, q - before, later - after)
+                through = c * (jnp.where(up, q, after) + part * minmod(first, step))
                 base[item, block, pair] = q - (through - side(through, 1))
         return carry
 
-    lax.fori_loop(0, COARSE, zonal, 0)
+    lax.fori_loop(0, COARSE, zonal, 0, unroll=2)
 
     ratio = jnp.concatenate([grid_ref[3], grid_ref[3]], axis=1)
     for order in range(WAVES):
@@ -287,8 +310,6 @@
         gain[16 * order : 16 * order + 8] = damping
         gain[16 * order + 8 : 16 * order + 16] = damping
 
-    has_below = jnp.where(band > 0, 1.0, 0.0)
-    has_above = jnp.where(band < bands - 1, 1.0, 0.0)
 
     def outer(a, b):
         return jnp.where(
@@ -300,7 +321,7 @@
 
     def slants(block, carry):
         a, b = own[1, block, 0], own[1, block, 1]
-        near = jnp.where(place < 2, from_down[1, block] * has_below, from_up[1, block] * has_above)
+        near = jnp.where(place < 2, from_down[1, block], from_up[1, block])
         winds = (a + down(a, -1), b + down(b, -1), near + outer(a, b))
         for index, wind in enumerate(winds):
             c = SPEED * wind
@@ -311,7 +332,7 @@
     def meridional(item):
         def one(block, carry):
             sign = jnp.where(place < 2, 1.0, -1.0)
-            low, high = from_down[0, block] * has_below, from_up[0, block] * has_above
+            low, high = from_down[0, block], from_up[0, block]
             cells = [own[0, block, 0], own[0, block, 1]]
             if item:
                 low, high = low * from_down[item, block], high * from_up[item, block]
@@ -356,7 +377,7 @@
                     field[block, rows] = value * inverse_h[block, rows]
             return carry
 
-        lax.fori_loop(0, COARSE, one, 0)
+        lax.fori_loop(0, COARSE, one, 0, unroll=2)
 
     def turn(item, step):
         target = lax.rem(group + step, GROUPS)
@@ -422,7 +443,7 @@
                     z_lo[spot] = (part - high.astype(jnp.float32)).astype(jnp.bfloat16)
             return carry
 
-        lax.fori_loop(0, 2, forward, 0)
+        lax.fori_loop(0, 2, forward, 0, unroll=True)
         damping = gain[...]
         waves = product(0) * jnp.concatenate([damping, damping], axis=1)
         high = waves.astype(jnp.bfloat16)
@@ -445,12 +466,15 @@
                 sent[item, block, :, lanes] = value
             return carry
 
-        lax.fori_loop(0, 2, backward, 0)
+        lax.fori_loop(0, 2, backward, 0, unroll=True)
 
     def end_halo(item):
-        for way in range(2):
-            halo(item, way).wait_recv()
-
+        pl.when(has_below)(lambda: halo(item, 0).wait_recv())
+        pl.when(has_above)(lambda: halo(item, 1).wait_recv())
+
+    drain_halo(0)
+    drain_halo(1)
+    start_halo(2)
     end_halo(0)
     end_halo(1)
     lax.fori_loop(0, COARSE, slants, 0)
@@ -460,8 +484,12 @@
         if item > 1:
             end_halo(item)
         meridional(item)
+        if item == 1:
+            drain_halo(2)
+            start_halo(3)
         polar(item)
         start_turn(item)
+    drain_halo(3)
 
     first_half = lax.broadcasted_iota(jnp.int32, (8, 128), 0) < ROWS
 
@@ -512,7 +540,7 @@
                 wide[pair, step] = total * target_ref[step, pair]
             return carry
 
-        lax.fori_loop(0, 2 * PER, one, 0)
+        lax.fori_loop(0, 2 * PER, one, 0, unroll=2)
 
     def pack(output):
         def one(pair, carry):
@@ -533,7 +561,7 @@
                 out_ref[output, pl.ds(2 * pair, 2), :, 128 * at : 128 * at + size] = value
             return carry
 
-        lax.fori_loop(0, 8, one, 0)
+        lax.fori_loop(0, 8, one, 0, unroll=True)
 
     end_turn(0)
     lax.fori_loop(0, 2 * PER, weigh, 0)
@@ -543,8 +571,6 @@
         gather(item)
         pack((0, 2, 1, 0)[item])
 
-    for copy in halos:
-        copy.wait_send()
     for item in range(4):
         for step in range(1, GROUPS):
             turn(item, step).wait_send()
@@ -555,8 +581,18 @@
 ):
     matrices, tables = constants()
     f32 = jnp.float32
-    hbm = pl.BlockSpec(memory_space=pl.ANY)
+    hbm = pl.BlockSpec(memory_space=pltpu.HBM)
     size = 16 * WAVES
+    operands = (
+        jnp.asarray(grid_table(lax.axis_size("lat"))),
+        reference_layer_shares,
+        zonal_velocity,
+        meridional_velocity,
+        heat_anomaly,
+        layer_pressure_depth,
+        jnp.asarray(matrices),
+        jnp.asarray(tables),
+    )
     result = pl.pallas_call(
         kernel,
         out_shape=jax.ShapeDtypeStruct((4, 16, ROWS, LON // GROUPS), f32),
@@ -594,21 +630,12 @@
             pltpu.SemaphoreType.DMA((4,)),
         ],
         compiler_params=pltpu.CompilerParams(
-            collective_id=0, has_side_effects=True, vmem_limit_bytes=56 << 20
+            collective_id=0, has_side_effects=True, vmem_limit_bytes=24 << 20
         ),
         cost_estimate=pl.CostEstimate(
             flops=2_000_000_000, bytes_accessed=4_000_000, transcendentals=0
         ),
-    )(
-        jnp.asarray(grid_table(lax.axis_size("lat"))),
-        reference_layer_shares,
-        zonal_velocity,
-        meridional_velocity,
-        heat_anomaly,
-        layer_pressure_depth,
-        jnp.asarray(matrices),
-        jnp.asarray(tables),
-    )
+    )(*(pltpu.with_memory_space_constraint(array, pltpu.HBM) for array in operands))
     return (result[0], result[1], result[2], result[3])
 
 

time: 35.8 us -> 32.3 us (0.902)
  Pallas kernels: 32.9 us -> 30.7 us
  local copies, waits for them, and re-layouts: 2.11 us -> 0.89 us
    pallas_call x1, Pallas kernels: 32.9 us -> 30.7 us  [on_device(): pl.pallas_call(kernel, out_shape=jax.ShapeDtypeStruct((4, 16, ROWS, LON /...]
    squeeze x1, local copies, waits for them, and re-layouts: 2.11 us -> 0.89 us  [on_device(): return (result[0], result[1], result[2], result[3])]
where the time goes in v2:
time: 32.3 us; the launch traced here: 32.2 us
  Pallas kernels  30.7 us (95%)
  local copies, waits for them, and re-layouts  0.89 us (3%)
  between operations  0.64 us (2%)
    pallas_call x1, Pallas kernels, on_device(): pl.pallas_call(kernel, out_shape=jax.ShapeDtypeStruct((4, 16, ROWS, LON /...  30.7 us
    squeeze x1, local copies, waits for them, and re-layouts, on_device(): return (result[0], result[1], result[2], result[3])  0.89 us

profile of v2, /device:TPU:1, one launch (start us, length us, event | category | flops | bytes accessed | tf_op | source)
XLA Modules:
  0.0 32.2 jit_solution(15179944656009323770)
XLA Ops:
  0.6 30.7 %shard_map.111 = f32[4,16,4,720]{3,2,1,0:T(4,128)S(1)} custom-call(f32[64,4,8,128]{3,2,1,0:T(8,128)} %constant.6.clone.grid_hbm, f32[16]{0:T(128)} %share_hbm.1, f32[4,4,2880]{2,1,0:T(4,128)} %u_hbm.1, f32[4,4,2880]{2,1,0:T(4,128)} %v_hbm.1, f32[4,4,2880]{2,1,0:T(4,128)} %t_hbm.1, f32[4,4,2880]{2,1,0:T(4,128)} %h_hbm.1, ...), custom_call_target="tpu_custom_call" | custom-call | flops 2000000000 | bytes 4000000 | tf_op jit(solution)/shard_map/pallas_call | solution.py:596
  31.3 0.9 %slice_bitcast_fusion = (f32[16,4,720]{2,1,0:T(4,128)}, f32[16,4,720]{2,1,0:T(4,128)}, f32[16,4,720]{2,1,0:T(4,128)}, f32[16,4,720]{2,1,0:T(4,128)}) fusion(f32[4,16,4,720]{3,2,1,0:T(4,128)S(1)} %shard_map.111), kind=kLoop, calls=%fused_computation | loop fusion | bytes 1474560 | tf_op jit(solution)/shard_map/squeeze | solution.py:639

commit v3 on v2

--- a/solution.py
+++ b/solution.py
@@ -21,6 +21,7 @@
 EDGE = 8
 PER = COARSE // GROUPS
 WAVES = COARSE // 2 + 1
+ORDER = (2, 3, 1, 0)
 MESH = pl.DeviceIdType.MESH
 
 
@@ -253,23 +254,27 @@
 
         lax.fori_loop(0, COARSE, edges, 0)
 
-    def halo(item, way):
+    def home(step):
+        return PER * lax.rem(group + step, GROUPS)
+
+    def halo(item, way, step):
+        spot = (item, pl.ds(home(step), PER)) if item < 2 else (item,)
         return pltpu.make_async_remote_copy(
-            src_ref=(to_down if way else to_up).at[item],
-            dst_ref=(from_up if way else from_down).at[item],
-            send_sem=halo_send.at[item, way],
-            recv_sem=halo_recv.at[item, way],
+            src_ref=(to_down if way else to_up).at[spot],
+            dst_ref=(from_up if way else from_down).at[spot],
+            send_sem=halo_send.at[item, way, step],
+            recv_sem=halo_recv.at[item, way, step],
             device_id=below if way else above,
             device_id_type=MESH,
         )
 
-    def start_halo(item):
-        pl.when(has_above)(lambda: halo(item, 0).start())
-        pl.when(has_below)(lambda: halo(item, 1).start())
-
-    def drain_halo(item):
-        pl.when(has_above)(lambda: halo(item, 0).wait_send())
-        pl.when(has_below)(lambda: halo(item, 1).wait_send())
+    def start_halo(item, step=0):
+        pl.when(has_above)(lambda: halo(item, 0, step).start())
+        pl.when(has_below)(lambda: halo(item, 1, step).start())
+
+    def drain_halo(item, step=0):
+        pl.when(has_above)(lambda: halo(item, 0, step).wait_send())
+        pl.when(has_below)(lambda: halo(item, 1, step).wait_send())
 
     for item in range(4):
         loads[item].wait()
@@ -279,8 +284,12 @@
                 barrier,
                 len(partners) + jnp.where(has_below, 1, 0) + jnp.where(has_above, 1, 0),
             )
-        if item < 2:
-            start_halo(item)
+        if item == 1:
+            for step in ORDER:
+                start_halo(0, step)
+                start_halo(1, step)
+        elif item == 2:
+            start_halo(2)
     for copy in tables:
         copy.wait()
 
@@ -302,6 +311,7 @@
 
     lax.fori_loop(0, COARSE, zonal, 0, unroll=2)
 
+    start_halo(3)
     ratio = jnp.concatenate([grid_ref[3], grid_ref[3]], axis=1)
     for order in range(WAVES):
         sine = jnp.broadcast_to(tab_ref[2, order : order + 1, :], (8, WIDE))
@@ -329,8 +339,11 @@
             lean_ref[block, 2 * index + 1] = limits(c)
         return carry
 
-    def meridional(item):
+    def meridional(item, step=None):
         def one(block, carry):
+            if step is not None:
+                block = home(step) + block
+                slants(block, carry)
             sign = jnp.where(place < 2, 1.0, -1.0)
             low, high = from_down[0, block], from_up[0, block]
             cells = [own[0, block, 0], own[0, block, 1]]
@@ -377,7 +390,10 @@
                     field[block, rows] = value * inverse_h[block, rows]
             return carry
 
-        lax.fori_loop(0, COARSE, one, 0, unroll=2)
+        if step is None:
+            lax.fori_loop(0, COARSE, one, 0, unroll=2)
+        else:
+            lax.fori_loop(0, PER, one, 0, unroll=True)
 
     def turn(item, step):
         target = lax.rem(group + step, GROUPS)
@@ -468,27 +484,28 @@
 
         lax.fori_loop(0, 2, backward, 0, unroll=True)
 
-    def end_halo(item):
-        pl.when(has_below)(lambda: halo(item, 0).wait_recv())
-        pl.when(has_above)(lambda: halo(item, 1).wait_recv())
-
-    drain_halo(0)
-    drain_halo(1)
-    start_halo(2)
-    end_halo(0)
-    end_halo(1)
-    lax.fori_loop(0, COARSE, slants, 0)
-    meridional(0)
-    start_turn(0)
+    def end_halo(item, step=0):
+        pl.when(has_below)(lambda: halo(item, 0, step).wait_recv())
+        pl.when(has_above)(lambda: halo(item, 1, step).wait_recv())
+
+    for step in ORDER:
+        end_halo(0, step)
+        end_halo(1, step)
+        meridional(0, step)
+        if step:
+            turn(0, step).start()
+        else:
+            keep(0).start()
     for item in range(1, 4):
         if item > 1:
             end_halo(item)
         meridional(item)
-        if item == 1:
-            drain_halo(2)
-            start_halo(3)
         polar(item)
         start_turn(item)
+    for step in ORDER:
+        drain_halo(0, step)
+        drain_halo(1, step)
+    drain_halo(2)
     drain_halo(3)
 
     first_half = lax.broadcasted_iota(jnp.int32, (8, 128), 0) < ROWS
@@ -623,8 +640,8 @@
             pltpu.VMEM((8, 2 * PER, 8, 128), f32),
             pltpu.VMEM((2 * PER, 8, 8, 128), f32),
             pltpu.SemaphoreType.DMA((8,)),
-            pltpu.SemaphoreType.DMA((4, 2)),
-            pltpu.SemaphoreType.DMA((4, 2)),
+            pltpu.SemaphoreType.DMA((4, 2, GROUPS)),
+            pltpu.SemaphoreType.DMA((4, 2, GROUPS)),
             pltpu.SemaphoreType.DMA((4, 3)),
             pltpu.SemaphoreType.DMA((4, 3)),
             pltpu.SemaphoreType.DMA((4,)),

time: 32.3 us -> 31.9 us (0.988)
  Pallas kernels: 30.7 us -> 30.2 us
    pallas_call x1, Pallas kernels: 30.7 us -> 30.2 us  [on_device(): pl.pallas_call(kernel, out_shape=jax.ShapeDtypeStruct((4, 16, ROWS, LON /...]
where the time goes in v3:
time: 31.9 us; the launch traced here: 31.8 us
  Pallas kernels  30.2 us (95%)
  local copies, waits for them, and re-layouts  0.89 us (3%)
  between operations  0.64 us (2%)
    pallas_call x1, Pallas kernels, on_device(): pl.pallas_call(kernel, out_shape=jax.ShapeDtypeStruct((4, 16, ROWS, LON /...  30.2 us
    squeeze x1, local copies, waits for them, and re-layouts, on_device(): return (result[0], result[1], result[2], result[3])  0.89 us

profile of v3, /device:TPU:1, one launch (start us, length us, event | category | flops | bytes accessed | tf_op | source)
XLA Modules:
  0.0 31.8 jit_solution(10837913865792077632)
XLA Ops:
  0.6 30.2 %shard_map.111 = f32[4,16,4,720]{3,2,1,0:T(4,128)S(1)} custom-call(f32[64,4,8,128]{3,2,1,0:T(8,128)} %constant.6.clone.grid_hbm, f32[16]{0:T(128)} %share_hbm.1, f32[4,4,2880]{2,1,0:T(4,128)} %u_hbm.1, f32[4,4,2880]{2,1,0:T(4,128)} %v_hbm.1, f32[4,4,2880]{2,1,0:T(4,128)} %t_hbm.1, f32[4,4,2880]{2,1,0:T(4,128)} %h_hbm.1, ...), custom_call_target="tpu_custom_call" | custom-call | flops 2000000000 | bytes 4000000 | tf_op jit(solution)/shard_map/pallas_call | solution.py:613
  30.9 0.9 %slice_bitcast_fusion = (f32[16,4,720]{2,1,0:T(4,128)}, f32[16,4,720]{2,1,0:T(4,128)}, f32[16,4,720]{2,1,0:T(4,128)}, f32[16,4,720]{2,1,0:T(4,128)}) fusion(f32[4,16,4,720]{3,2,1,0:T(4,128)S(1)} %shard_map.111), kind=kLoop, calls=%fused_computation | loop fusion | bytes 1474560 | tf_op jit(solution)/shard_map/squeeze | solution.py:656

commit v4 on v3

--- a/solution.py
+++ b/solution.py
@@ -202,7 +202,7 @@
         pltpu.make_async_copy(share_hbm, share_ref, in_sem.at[6]),
         pltpu.make_async_copy(mat_hbm, mat_ref, in_sem.at[7]),
     ]
-    for copy in loads + tables:
+    for copy in loads + tables[:3]:
         copy.start()
 
     @pl.when(jnp.logical_not(has_below))
@@ -285,6 +285,7 @@
                 len(partners) + jnp.where(has_below, 1, 0) + jnp.where(has_above, 1, 0),
             )
         if item == 1:
+            tables[3].start()
             for step in ORDER:
                 start_halo(0, step)
                 start_halo(1, step)

time: 31.9 us -> 31.9 us (level)
  no operation moved by 1% of the time
where the time goes in v4:
time: 31.9 us; the launch traced here: 31.8 us
  Pallas kernels  30.2 us (95%)
  local copies, waits for them, and re-layouts  0.89 us (3%)
  between operations  0.64 us (2%)
    pallas_call x1, Pallas kernels, on_device(): pl.pallas_call(kernel, out_shape=jax.ShapeDtypeStruct((4, 16, ROWS, LON /...  30.2 us
    squeeze x1, local copies, waits for them, and re-layouts, on_device(): return (result[0], result[1], result[2], result[3])  0.89 us

profile of v4, /device:TPU:1, one launch (start us, length us, event | category | flops | bytes accessed | tf_op | source)
XLA Modules:
  0.0 31.8 jit_solution(16396887571425615948)
XLA Ops:
  0.6 30.2 %shard_map.111 = f32[4,16,4,720]{3,2,1,0:T(4,128)S(1)} custom-call(f32[64,4,8,128]{3,2,1,0:T(8,128)} %constant.6.clone.grid_hbm, f32[16]{0:T(128)} %share_hbm.1, f32[4,4,2880]{2,1,0:T(4,128)} %u_hbm.1, f32[4,4,2880]{2,1,0:T(4,128)} %v_hbm.1, f32[4,4,2880]{2,1,0:T(4,128)} %t_hbm.1, f32[4,4,2880]{2,1,0:T(4,128)} %h_hbm.1, ...), custom_call_target="tpu_custom_call" | custom-call | flops 2000000000 | bytes 4000000 | tf_op jit(solution)/shard_map/pallas_call | solution.py:614
  30.9 0.9 %slice_bitcast_fusion = (f32[16,4,720]{2,1,0:T(4,128)}, f32[16,4,720]{2,1,0:T(4,128)}, f32[16,4,720]{2,1,0:T(4,128)}, f32[16,4,720]{2,1,0:T(4,128)}) fusion(f32[4,16,4,720]{3,2,1,0:T(4,128)S(1)} %shard_map.111), kind=kLoop, calls=%fused_computation | loop fusion | bytes 1474560 | tf_op jit(solution)/shard_map/squeeze | solution.py:657

commit v5 on v3

--- a/solution.py
+++ b/solution.py
@@ -179,7 +179,9 @@
     group = lax.axis_index("lev")
     above = (lax.rem(band + 1, bands), group)
     below = (lax.rem(band + bands - 1, bands), group)
-    partners = [(band, lax.rem(group + step, GROUPS)) for step in range(1, GROUPS)]
+    beside = group + 1 - 2 * lax.rem(group, 2)
+    groups = (group, beside, lax.rem(group + 2, GROUPS), lax.rem(beside + 2, GROUPS))
+    partners = [(band, groups[step]) for step in range(1, GROUPS)]
 
     has_below, has_above = band > 0, band < bands - 1
     barrier = pltpu.get_barrier_semaphore()
@@ -255,7 +257,7 @@
         lax.fori_loop(0, COARSE, edges, 0)
 
     def home(step):
-        return PER * lax.rem(group + step, GROUPS)
+        return PER * groups[step]
 
     def halo(item, way, step):
         spot = (item, pl.ds(home(step), PER)) if item < 2 else (item,)
@@ -396,7 +398,7 @@
             lax.fori_loop(0, PER, one, 0, unroll=True)
 
     def turn(item, step):
-        target = lax.rem(group + step, GROUPS)
+        target = groups[step]
         return pltpu.make_async_remote_copy(
             src_ref=sent.at[item, pl.ds(PER * target, PER)],
             dst_ref=held.at[item, group],
@@ -418,7 +420,7 @@
 
     def end_turn(item):
         for step in range(1, GROUPS):
-            source = lax.rem(group + GROUPS - step, GROUPS)
+            source = groups[step]
             pltpu.make_async_remote_copy(
                 src_ref=sent.at[item, pl.ds(0, PER)],
                 dst_ref=held.at[item, source],

time: 31.9 us -> 31.9 us (level)
  no operation moved by 1% of the time
where the time goes in v5:
time: 31.9 us; the launch traced here: 31.8 us
  Pallas kernels  30.2 us (95%)
  local copies, waits for them, and re-layouts  0.89 us (3%)
  between operations  0.64 us (2%)
    pallas_call x1, Pallas kernels, on_device(): pl.pallas_call(kernel, out_shape=jax.ShapeDtypeStruct((4, 16, ROWS, LON /...  30.2 us
    squeeze x1, local copies, waits for them, and re-layouts, on_device(): return (result[0], result[1], result[2], result[3])  0.89 us

profile of v5, /device:TPU:1, one launch (start us, length us, event | category | flops | bytes accessed | tf_op | source)
XLA Modules:
  0.0 31.8 jit_solution(14219958371515644061)
XLA Ops:
  0.6 30.2 %shard_map.111 = f32[4,16,4,720]{3,2,1,0:T(4,128)S(1)} custom-call(f32[64,4,8,128]{3,2,1,0:T(8,128)} %constant.6.clone.grid_hbm, f32[16]{0:T(128)} %share_hbm.1, f32[4,4,2880]{2,1,0:T(4,128)} %u_hbm.1, f32[4,4,2880]{2,1,0:T(4,128)} %v_hbm.1, f32[4,4,2880]{2,1,0:T(4,128)} %t_hbm.1, f32[4,4,2880]{2,1,0:T(4,128)} %h_hbm.1, ...), custom_call_target="tpu_custom_call" | custom-call | flops 2000000000 | bytes 4000000 | tf_op jit(solution)/shard_map/pallas_call | solution.py:615
  30.9 0.9 %slice_bitcast_fusion = (f32[16,4,720]{2,1,0:T(4,128)}, f32[16,4,720]{2,1,0:T(4,128)}, f32[16,4,720]{2,1,0:T(4,128)}, f32[16,4,720]{2,1,0:T(4,128)}) fusion(f32[4,16,4,720]{3,2,1,0:T(4,128)S(1)} %shard_map.111), kind=kLoop, calls=%fused_computation | loop fusion | bytes 1474560 | tf_op jit(solution)/shard_map/squeeze | solution.py:658
